TPU v7x, 128 devices: a whole 4x4x4 slice. The times are simulated.
128 devices in a mesh: ctx: 64 (over z, y, x), head: 2 (over core).
Axes of the slice: x: 4, y: 4, z: 4, core: 2. Of those that a mesh axis runs over, the one named last changes fastest.
Arguments:
- queries: bfloat16 [16384, 4096], P('ctx', 'head'), may hold values from -6 to 6
- keys: bfloat16 [16384, 4096], P('ctx', 'head'), may hold values from -6 to 6
- values: bfloat16 [16384, 4096], P('ctx', 'head'), may hold values from -6 to 6
- log_decay: float32 [32, 16384], P('head', 'ctx'), may hold values from -0.8 to 0, as said below
- norm_gain: float32 [4096], P('head'), may hold values from 0.1 to 1.9
- d_out: bfloat16 [16384, 4096], P('ctx', 'head'), may hold values from -6 to 6
Outputs:
- output: bfloat16 [16384, 4096], P('ctx', 'head')
- grad_queries: bfloat16 [16384, 4096], P('ctx', 'head')
- grad_keys: bfloat16 [16384, 4096], P('ctx', 'head')
- grad_values: bfloat16 [16384, 4096], P('ctx', 'head')
Inputs may be any that keep to these rules, and one draw needn't show every extreme that they name: log_decay is negative everywhere.
All inputs are finite; a program needn't handle non-finite values.
Results may differ from a plain program's by a relative error of at most 0.014.
Values may be sent and summed in bfloat16 or wider, within the bound.
A program may use at most 192 MiB of HBM per device.

v0:
```python
import jax
import jax.numpy as jnp
from jax import lax
from jax.sharding import PartitionSpec as P

DH = 128


EPSILON = 1e-06


def carried_in(part, axis, combine, identity, reverse):
    count = lax.axis_size(axis)
    place = lax.axis_index(axis)
    ahead = count - 1 - place if reverse else place
    gathered = jax.tree.map(lambda a: lax.all_gather(a, axis), part)
    state = jax.tree.map(lambda a, e: jnp.zeros_like(a) + jnp.asarray(e, a.dtype), part, identity)

    def one(lap, state):
        source = count - 1 - lap if reverse else lap
        return combine(
            state, jax.tree.map(lambda a: lax.dynamic_index_in_dim(a, source, 0, False), gathered)
        )

    return lax.fori_loop(0, ahead, one, state)


def decay_matrix(cumulative):
    length_here = cumulative.shape[-1]
    rows_index = jnp.arange(length_here)[:, None]
    cols_index = jnp.arange(length_here)[None, :]
    spread = cumulative[:, :, None] - cumulative[:, None, :]
    return jnp.exp(jnp.where(rows_index >= cols_index, spread, -1e30))


def forward_combine(earlier, later):
    return (earlier[0] * later[0], later[0][:, None, None] * earlier[1] + later[1])


def reverse_combine(earlier, later):
    return (later[0] * earlier[0], later[1] + later[0][:, None, None] * earlier[1])


def local(queries, keys, values, log_decay, norm_gain, d_out):
    positions, full_width = queries.shape
    head_count = full_width // DH

    def split_heads(array):
        return array.reshape(positions, head_count, DH).transpose(1, 0, 2)

    def join_heads(array):
        return array.transpose(1, 0, 2).reshape(positions, full_width)

    query_h = split_heads(queries)
    key_h = split_heads(keys)
    value_h = split_heads(values)
    cumulative = jnp.cumsum(log_decay, axis=1)
    lead = jnp.exp(cumulative)[:, :, None]
    trail = jnp.exp(cumulative[:, -1:] - cumulative)[:, :, None]
    block_decay = jnp.exp(cumulative[:, -1])
    decay = decay_matrix(cumulative)
    decayed_keys = (key_h.astype(jnp.float32) * trail).astype(jnp.bfloat16)
    own_state = jnp.einsum(
        "htd,hte->hde", decayed_keys, value_h, preferred_element_type=jnp.float32
    )
    identity = (jnp.ones_like(block_decay), jnp.zeros_like(own_state))
    entering_low = carried_in((block_decay, own_state), "ctx", forward_combine, identity, False)[
        1
    ].astype(jnp.bfloat16)
    scores = jnp.einsum("htd,hsd->hts", query_h, key_h, preferred_element_type=jnp.float32)
    weights = (scores * decay).astype(jnp.bfloat16)
    attn = lead * jnp.einsum(
        "htd,hde->hte", query_h, entering_low, preferred_element_type=jnp.float32
    )
    attn = attn + jnp.einsum("hts,hse->hte", weights, value_h, preferred_element_type=jnp.float32)
    full_features = head_count * DH * lax.axis_size("head")
    squares = lax.psum(jnp.sum(attn * attn, axis=(0, 2)), "head")
    scale = lax.rsqrt(squares / full_features + EPSILON)[None, :, None]
    normed = attn * scale
    gain = norm_gain.reshape(head_count, DH)[:, None, :]
    output = join_heads((normed * gain).astype(jnp.bfloat16))
    grad_gain = gain * split_heads(d_out).astype(jnp.float32)
    inner_sum = lax.psum(jnp.sum(normed * grad_gain, axis=(0, 2)), "head")
    d_attn = (scale * (grad_gain - normed * (inner_sum / full_features)[None, :, None])).astype(
        jnp.bfloat16
    )
    decayed_queries = (query_h.astype(jnp.float32) * lead).astype(jnp.bfloat16)
    own_grad = jnp.einsum(
        "htd,hte->hde", decayed_queries, d_attn, preferred_element_type=jnp.float32
    )
    leaving_low = carried_in((block_decay, own_grad), "ctx", reverse_combine, identity, True)[
        1
    ].astype(jnp.bfloat16)
    grad_weights = (
        jnp.einsum("htd,hsd->hts", d_attn, value_h, preferred_element_type=jnp.float32) * decay
    ).astype(jnp.bfloat16)
    grad_query = lead * jnp.einsum(
        "hte,hde->htd", d_attn, entering_low, preferred_element_type=jnp.float32
    )
    grad_query = grad_query + jnp.einsum(
        "hts,hsd->htd", grad_weights, key_h, preferred_element_type=jnp.float32
    )
    grad_key = trail * jnp.einsum(
        "hte,hde->htd", value_h, leaving_low, preferred_element_type=jnp.float32
    )
    grad_key = grad_key + jnp.einsum(
        "hts,htd->hsd", grad_weights, query_h, preferred_element_type=jnp.float32
    )
    grad_value = trail * jnp.einsum(
        "htd,hde->hte", key_h, leaving_low, preferred_element_type=jnp.float32
    )
    grad_value = grad_value + jnp.einsum(
        "hts,hte->hse", weights, d_attn, preferred_element_type=jnp.float32
    )
    return (
        output,
        join_heads(grad_query.astype(jnp.bfloat16)),
        join_heads(grad_key.astype(jnp.bfloat16)),
        join_heads(grad_value.astype(jnp.bfloat16)),
    )


def solution(mesh):
    placed = (
        P("ctx", "head"),
        P("ctx", "head"),
        P("ctx", "head"),
        P("head", "ctx"),
        P("head"),
        P("ctx", "head"),
    )
    return jax.shard_map(
        local,
        mesh=mesh,
        in_specs=placed,
        out_specs=(P("ctx", "head"), P("ctx", "head"), P("ctx", "head"), P("ctx", "head")),
        check_vma=False,
    )
```

profile of v0, /device:TPU:0, one launch (start us, length us, event | category | flops | bytes accessed | tf_op | source)
XLA Modules:
  0.0 791.9 jit_solution(12316669435714325841)
XLA Ops:
  9.0 3.9 fusion.9
  13.0 1.6 copy.106
  16.2 182.8 %all-reduce = f32[1024]{0:T(1024)S(1)} all-reduce(f32[1024]{0:T(1024)S(1)} %dynamic-update-slice), channel_id=2, replica_groups=mesh['ctx'=64,'head'=2] {'ctx'}, use_global_device_ids=true, to_apply=%add | all-reduce | flops 1024 | bytes 8192
  200.4 1.6 copy.86
  202.0 2.4 multiply_convert_fusion.1
  204.5 89.7 %all-gather.6.cloned.1.call-done = f32[1024,128,128]{2,1,0:T(8,128)} async-done(((f32[16,128,128]{2,1,0:T(8,128)}), f32[1024,128,128]{2,1,0:T(8,128)}) %all-gather.6.cloned.1.call-update) | async-done | bytes 67108880 | tf_op jit(solution)/shard_map/all_gather | solution.py:16
  294.3 1.9 fusion.26
  296.4 2.9 multiply_reduce_fusion
  299.4 2.4 psum.14
  301.8 2.6 fusion.3
  304.4 2.5 psum.15
  306.9 2.7 fusion.5
  312.1 2.4 copy.116
  314.5 3.0 fusion.8
  317.5 2.4 copy.92
  324.6 3.5 fusion.29
  328.1 1.8 fusion.30
  329.9 350.8 %all-gather.8.cloned.1.call-done = f32[1024,128,128]{2,1,0:T(8,128)} async-done(((f32[16,128,128]{2,1,0:T(8,128)}), f32[1024,128,128]{2,1,0:T(8,128)}) %all-gather.8.cloned.1.call-update) | async-done | bytes 67108880 | tf_op jit(solution)/shard_map/all_gather | solution.py:16
  680.8 94.2 %while.27 = (s32[]{:T(128)}, f32[16,128,128]{2,1,0:T(8,128)S(1)}, s32[]{:T(128)}, f32[64,16,128,128]{3,2,1,0:T(8,128)}, f32[64,16]{1,0:T(8,128)S(1)}, /*index=5*/s32[]{:T(128)}, s32[]{:T(128)}, s32[]{:T(128)}, s32[]{:T(128)}) while((s32[]{:T(128)}, f32[16,128,128]{2,1,0:T(8,128)S(1)}, s32[]{:T(128)}, f32[64,16,128,128]{3,2,1,0:T(8,128)}, ...), condition=%wide.region_9.10_spmd, body=%wide.region_8.9_spmd.sunk | while | flops 524294 | bytes 3146075 | solution.py:25
  680.9 1.6 bitcast_add_fusion.11
  684.0 1.4 bitcast_add_fusion.11
  687.0 1.4 bitcast_add_fusion.11
  690.0 1.4 bitcast_add_fusion.11
  694.4 1.4 bitcast_add_fusion.11
  697.4 1.4 bitcast_add_fusion.11
  700.4 1.4 bitcast_add_fusion.11
  704.9 1.4 bitcast_add_fusion.11
  707.9 1.4 bitcast_add_fusion.11
  712.4 1.4 bitcast_add_fusion.11
  715.3 1.4 bitcast_add_fusion.11
  718.3 1.4 bitcast_add_fusion.11
  722.8 1.4 bitcast_add_fusion.11
  725.8 1.4 bitcast_add_fusion.11
  728.8 1.4 bitcast_add_fusion.11
  733.3 1.4 bitcast_add_fusion.11
  736.2 1.4 bitcast_add_fusion.11
  740.7 1.4 bitcast_add_fusion.11
  743.7 1.4 bitcast_add_fusion.11
  746.7 1.4 bitcast_add_fusion.11
  751.2 1.4 bitcast_add_fusion.11
  754.2 1.4 bitcast_add_fusion.11
  757.1 1.4 bitcast_add_fusion.11
  761.6 1.4 bitcast_add_fusion.11
  764.6 1.4 bitcast_add_fusion.11
  775.0 2.7 fusion.1
  777.7 2.4 copy.94
  780.1 2.7 fusion
  782.8 2.3 copy.95
  (167 shorter events, 67.4 us)
Async XLA Ops:
  7.2 0.7 copy-start
  7.2 287.0 %all-gather.6.cloned.1.call-start = ((), (), s32[]{:S(2)}) async-start(), calls=%async_computation | async-start | bytes 68157440 | tf_op jit(solution)/shard_map/all_gather | solution.py:16
  12.9 1.7 copy-start.18
  12.9 186.2 %copy-start.11 = (bf16[256,2048]{1,0:T(8,128)(2,1)S(1)}, bf16[256,2048]{1,0:T(8,128)(2,1)}, u32[]{:S(2)}) copy-start(bf16[256,2048]{1,0:T(8,128)(2,1)} %param.12) | copy-start | bytes 3145732
  12.9 667.8 %all-gather.8.cloned.1.call-start = ((), (), s32[]{:S(2)}) async-start(), calls=%async_computation.1 | async-start | bytes 68157440 | tf_op jit(solution)/shard_map/all_gather | solution.py:16
  13.0 187.4 %copy-start.16 = (bf16[256,2048]{1,0:T(8,128)(2,1)S(1)}, bf16[256,2048]{1,0:T(8,128)(2,1)}, u32[]{:S(2)}) copy-start(bf16[256,2048]{1,0:T(8,128)(2,1)} %param.15) | copy-start | bytes 3145732
  14.6 187.4 %copy-start.3 = (bf16[256,2048]{0,1:T(8,128)(2,1)}, bf16[256,2048]{0,1:T(8,128)(2,1)S(1)}, u32[]{:S(2)}) copy-start(bf16[256,2048]{0,1:T(8,128)(2,1)S(1)} %copy.106) | copy-start | bytes 3145732
  200.4 1.7 copy-start.13
  294.3 1.9 copy-start.6
  294.3 2.2 copy-start.14
  296.4 5.4 copy-start.17
  306.9 3.7 copy-start.4
  309.6 1.0 copy-start.1
  317.5 2.4 copy-start.2
  317.5 2.4 copy-start.12
  319.9 1.5 copy-start.15
  321.3 1.3 copy-start.10
  323.1 1.4 copy-start.5
  324.6 3.5 copy-start.7
  680.8 94.2 %copy-start.9 = (f32[16,256,128]{1,2,0:T(8,128)S(1)}, f32[16,256,128]{1,2,0:T(8,128)}, u32[]{:S(2)}) copy-start(f32[16,256,128]{1,2,0:T(8,128)} %fusion.29) | copy-start | bytes 6291460
  777.7 2.4 copy-start.8
Sparse Core Ops, SparseCore 0:
  13.0 281.0 all-gather.5
  312.2 368.4 all-gather.7
where the time goes:
time: 796 us; the launch traced here: 792 us
  waiting for transfers between devices  441 us (55%)
  blocking collectives  188 us (24%)
  other arithmetic  100 us (13%)
  matrix products  25.9 us (3%)
  local copies, waits for them, and re-layouts  20.1 us (3%)
  between operations  14.9 us (2%)
    all_gather x2, waiting for transfers between devices, carried_in(): gathered = jax.tree.map(lambda a: lax.all_gather(a, axis), part)  440 us
    unnamed x1, blocking collectives  183 us
    add x63, other arithmetic, reverse_combine(): later[1] + later[0][:, None, None] * earlier[1]  91.3 us
  transfers between devices with their start and end apart: 2, of which 2 were waited for; matrix products, arithmetic and copies ran while one was open for 3% of the time, Pallas kernels for 0%

commit v1 on v0

v1 whole, which is shorter than its diff:
```python
import functools

import jax
import jax.numpy as jnp
from jax import lax
from jax.experimental import pallas as pl
from jax.experimental.pallas import tpu as pltpu
from jax.sharding import PartitionSpec as P

DH = 128
EPSILON = 1e-06
MESH = pl.DeviceIdType.MESH
F32 = jnp.float32
BF16 = jnp.bfloat16


def dot(a, b, dims):
    return lax.dot_general(a, b, (dims, ((), ())), preferred_element_type=F32)


NN = ((1,), (0,))
NT = ((1,), (1,))
TN = ((0,), (0,))


def kernel(
    n, heads, pos,
    q_hbm, k_hbm, v_hbm, ld_hbm, gain_hbm, g_hbm,
    out_hbm, gq_hbm, gk_hbm, gv_hbm,
    q, k, v, g, ld, gain,
    cum, cumb, leadb, trailb, decay, weights, dk, ql,
    attn, d_attn, out, gq, gk, gv,
    s_send, s_recv, e_send, e_recv, t_send, t_recv, l_send, l_recv,
    totals, block_decay, sums, sums_in,
    in_sem, out_sem, sems, sum_sem,
):
    c = lax.axis_index("ctx")
    core = lax.axis_index("head")
    rows = DH * heads // n
    per_head = n // heads
    side = 8
    c_hi, c_lo = c // side, c % side
    width = heads * DH

    loads = [
        pltpu.make_async_copy(src, dst, in_sem.at[i])
        for i, (src, dst) in enumerate(
            ((ld_hbm, ld), (k_hbm, k), (v_hbm, v), (q_hbm, q), (gain_hbm, gain), (g_hbm, g))
        )
    ]
    for load in loads:
        load.start()

    barrier = pltpu.get_barrier_semaphore()

    def greet(i, _):
        pl.semaphore_signal(
            barrier, inc=1, device_id=((c + i) % n, core), device_id_type=MESH
        )
        return 0

    lax.fori_loop(1, n, greet, 0)
    pl.semaphore_signal(barrier, inc=1, device_id=(c, 1 - core), device_id_type=MESH)

    def lanes(h):
        return pl.ds(pl.multiple_of(h * DH, DH), DH)

    def share_copy(src, dst, which, dest):
        return pltpu.make_async_remote_copy(
            src_ref=src.at[dest],
            dst_ref=dst.at[c],
            send_sem=sems.at[2 * which],
            recv_sem=sems.at[2 * which + 1],
            device_id=(dest, core),
            device_id_type=MESH,
        )

    def send_shares(src, dst, which):
        def one(i, _):
            share_copy(src, dst, which, (c + i) % n).start()
            return 0

        lax.fori_loop(1, n, one, 0)
        dst[c] = src[c]

    def all_shares(src, dst, which):
        return pltpu.make_async_remote_copy(
            src_ref=src.at[pl.ds(0, n - 1)],
            dst_ref=dst.at[pl.ds(0, n - 1)],
            send_sem=sems.at[2 * which],
            recv_sem=sems.at[2 * which + 1],
            device_id=((c + 1) % n, core),
            device_id_type=MESH,
        )

    loads[0].wait()
    t_i = lax.broadcasted_iota(jnp.int32, (pos, pos), 0)
    s_i = lax.broadcasted_iota(jnp.int32, (pos, pos), 1)
    lower = jnp.where(t_i >= s_i, 1.0, 0.0).astype(BF16)
    ld_all = jnp.concatenate([ld[...], jnp.zeros((DH - heads, pos), F32)], axis=0)
    hi = ld_all.astype(BF16)
    rest = ld_all - hi.astype(F32)
    mid = rest.astype(BF16)
    low = (rest - mid.astype(F32)).astype(BF16)
    cum_t = dot(lower, hi, NT) + dot(lower, mid, NT) + dot(lower, low, NT)
    cum_h = dot(hi, lower, NT) + dot(mid, lower, NT) + dot(low, lower, NT)
    cum[...] = cum_h[:heads]
    last = cum_t[pos - 1 : pos, :]
    trail_t = jnp.exp(last - cum_t)
    for h in range(heads):
        trailb[h] = jnp.broadcast_to(trail_t[:, h : h + 1], (pos, DH))
    totals[c_hi, c_lo] = last

    loads[1].wait()
    loads[2].wait()

    def own_state(h, _):
        keys = (k[:, lanes(h)].astype(F32) * trailb[h]).astype(BF16)
        dk[:, lanes(h)] = keys
        state = dot(keys, v[:, lanes(h)], TN).astype(BF16)
        s_send[pl.ds(h * per_head, per_head)] = state.reshape(per_head, rows, DH)
        return 0

    lax.fori_loop(0, heads, own_state, 0, unroll=2)

    pl.semaphore_wait(barrier, n)

    def totals_row(i):
        return pltpu.make_async_remote_copy(
            src_ref=totals.at[c_hi, c_lo],
            dst_ref=totals.at[c_hi, c_lo],
            send_sem=sum_sem.at[2],
            recv_sem=sum_sem.at[3],
            device_id=(c_hi * side + (c_lo + i) % side, core),
            device_id_type=MESH,
        )

    def totals_rows(i):
        return pltpu.make_async_remote_copy(
            src_ref=totals.at[c_hi],
            dst_ref=totals.at[c_hi],
            send_sem=sum_sem.at[4],
            recv_sem=sum_sem.at[5],
            device_id=(((c_hi + i) % side) * side + c_lo, core),
            device_id_type=MESH,
        )

    for i in range(1, side):
        totals_row(i).start()
    send_shares(s_send, s_recv, 0)

    lead_t = jnp.exp(cum_t)
    for h in range(heads):
        cumb[h] = jnp.broadcast_to(cum_t[:, h : h + 1], (pos, DH))
        leadb[h] = jnp.broadcast_to(lead_t[:, h : h + 1], (pos, DH))

    some = pltpu.make_async_remote_copy(
        src_ref=totals.at[0, pl.ds(0, side - 1)],
        dst_ref=totals.at[0, pl.ds(0, side - 1)],
        send_sem=sum_sem.at[2],
        recv_sem=sum_sem.at[3],
        device_id=((c + 1) % n, core),
        device_id_type=MESH,
    )
    some.wait()
    for i in range(1, side):
        totals_rows(i).start()

    loads[3].wait()

    def inside(h, _):
        scores = dot(q[:, lanes(h)], k[:, lanes(h)], NT)
        row = cum[pl.ds(h, 1), :]
        col = cumb[h]
        spread = jnp.concatenate([col, col], axis=1) - row
        d = jnp.exp(jnp.where(t_i >= s_i, spread, -1e30))
        decay[h] = d
        w = (scores * d).astype(BF16)
        weights[h] = w
        attn[:, lanes(h)] = dot(w, v[:, lanes(h)], NN)
        ql[:, lanes(h)] = (q[:, lanes(h)].astype(F32) * leadb[h]).astype(BF16)
        return 0

    lax.fori_loop(0, heads, inside, 0, unroll=2)

    some = pltpu.make_async_remote_copy(
        src_ref=totals.at[pl.ds(0, side - 1)],
        dst_ref=totals.at[pl.ds(0, side - 1)],
        send_sem=sum_sem.at[4],
        recv_sem=sum_sem.at[5],
        device_id=((c + 1) % n, core),
        device_id_type=MESH,
    )
    some.wait()
    every = totals[...].reshape(n, DH)
    lane_i = lax.broadcasted_iota(jnp.int32, (n, DH), 1)
    mine = jnp.sum(jnp.where(lane_i == c // per_head, every, 0.0), axis=1, keepdims=True)
    block_decay[...] = jnp.broadcast_to(jnp.exp(mine), (n, DH))

    def scan(src, dst, reverse):
        def one(i, state):
            j = n - 1 - i if reverse else i
            dst[j] = state.astype(BF16)
            return state * block_decay[pl.ds(j, 1), :] + src[j].astype(F32)

        lax.fori_loop(0, n, one, jnp.zeros((rows, DH), F32), unroll=8)

    all_shares(s_send, s_recv, 0).wait()
    scan(s_recv, e_send, False)
    send_shares(e_send, e_recv, 1)
    loads[4].wait()
    loads[5].wait()
    all_shares(e_send, e_recv, 1).wait()

    def attend(h, carry):
        squares, inner = carry
        entering = e_recv[pl.ds(h * per_head, per_head)].reshape(DH, DH)
        a = attn[:, lanes(h)] + leadb[h] * dot(q[:, lanes(h)], entering, NN)
        attn[:, lanes(h)] = a
        gg = gain[:, lanes(h)] * g[:, lanes(h)].astype(F32)
        return squares + a * a, inner + a * gg

    zero = jnp.zeros((pos, DH), F32)
    squares, inner = lax.fori_loop(0, heads, attend, (zero, zero), unroll=2)
    squares = jnp.sum(squares, axis=1, keepdims=True)
    inner = jnp.sum(inner, axis=1, keepdims=True)
    half_i = lax.broadcasted_iota(jnp.int32, (pos, DH), 1)
    sums[...] = jnp.where(half_i < DH // 2, squares, inner)
    swap = pltpu.make_async_remote_copy(
        src_ref=sums,
        dst_ref=sums_in,
        send_sem=sum_sem.at[0],
        recv_sem=sum_sem.at[1],
        device_id=(c, 1 - core),
        device_id_type=MESH,
    )
    swap.start()
    swap.wait()
    both = sums[...] + sums_in[...]
    full = 2 * width
    scale = lax.rsqrt(both[:, 0:1] / full + EPSILON)
    pull = scale * scale * (both[:, DH - 1 : DH] / full)
    scale = jnp.broadcast_to(scale, (pos, DH))
    pull = jnp.broadcast_to(pull, (pos, DH))
    sums[...] = scale

    def own_grad(h, _):
        a = attn[:, lanes(h)]
        gg = gain[:, lanes(h)] * g[:, lanes(h)].astype(F32)
        d = (scale * (gg - a * pull)).astype(BF16)
        d_attn[:, lanes(h)] = d
        state = dot(ql[:, lanes(h)], d, TN).astype(BF16)
        t_send[pl.ds(h * per_head, per_head)] = state.reshape(per_head, rows, DH)
        return 0

    lax.fori_loop(0, heads, own_grad, 0, unroll=2)
    send_shares(t_send, t_recv, 2)

    def gradients(h, _):
        d = d_attn[:, lanes(h)]
        out[:, lanes(h)] = (attn[:, lanes(h)] * sums[...] * gain[:, lanes(h)]).astype(BF16)
        w = weights[h]
        gw = (dot(d, v[:, lanes(h)], NT) * decay[h]).astype(BF16)
        entering = e_recv[pl.ds(h * per_head, per_head)].reshape(DH, DH)
        gq[:, lanes(h)] = (
            leadb[h] * dot(d, entering, NT) + dot(gw, k[:, lanes(h)], NN)
        ).astype(BF16)
        attn[:, lanes(h)] = dot(gw, q[:, lanes(h)], TN)
        decay[h, :, 0:DH] = dot(w, d, TN)
        return 0

    lax.fori_loop(0, heads // 2, gradients, 0)
    all_shares(t_send, t_recv, 2).wait()
    scan(t_recv, l_send, True)
    send_shares(l_send, l_recv, 3)
    lax.fori_loop(heads // 2, heads, gradients, 0)
    stores = [
        pltpu.make_async_copy(src, dst, out_sem.at[i])
        for i, (src, dst) in enumerate(
            ((out, out_hbm), (gq, gq_hbm), (gk, gk_hbm), (gv, gv_hbm))
        )
    ]
    stores[0].start()
    stores[1].start()
    all_shares(l_send, l_recv, 3).wait()

    def finish(h, _):
        leaving = l_recv[pl.ds(h * per_head, per_head)].reshape(DH, DH)
        gk[:, lanes(h)] = (
            attn[:, lanes(h)] + trailb[h] * dot(v[:, lanes(h)], leaving, NT)
        ).astype(BF16)
        gv[:, lanes(h)] = (
            decay[h, :, 0:DH] + trailb[h] * dot(k[:, lanes(h)], leaving, NN)
        ).astype(BF16)
        return 0

    lax.fori_loop(0, heads, finish, 0, unroll=2)
    stores[2].start()
    stores[3].start()
    for store in stores:
        store.wait()


def solution(mesh):
    n = mesh.shape["ctx"]

    def local(queries, keys, values, log_decay, norm_gain, d_out):
        pos, width = queries.shape
        heads = width // DH
        rows = DH * heads // n
        wide = jax.ShapeDtypeStruct((pos, width), BF16)
        anywhere = pl.BlockSpec(memory_space=pl.ANY)
        shares = pltpu.VMEM((n, rows, DH), BF16)
        columns = pltpu.VMEM((heads, pos, DH), F32)
        flat = pltpu.VMEM((pos, width), BF16)
        return pl.pallas_call(
            functools.partial(kernel, n, heads, pos),
            out_shape=[wide] * 4,
            in_specs=[anywhere] * 6,
            out_specs=[anywhere] * 4,
            scratch_shapes=[
                flat, flat, flat, flat,
                pltpu.VMEM((heads, pos), F32),
                pltpu.VMEM((1, width), F32),
                pltpu.VMEM((heads, pos), F32),
                columns, columns, columns,
                pltpu.VMEM((heads, pos, pos), F32),
                pltpu.VMEM((heads, pos, pos), BF16),
                flat, flat,
                pltpu.VMEM((pos, width), F32),
                flat, flat, flat, flat, flat,
                shares, shares, shares, shares, shares, shares, shares, shares,
                pltpu.VMEM((8, n // 8, 1, DH), F32),
                pltpu.VMEM((n, DH), F32),
                pltpu.VMEM((pos, DH), F32),
                pltpu.VMEM((pos, DH), F32),
                pltpu.SemaphoreType.DMA((6,)),
                pltpu.SemaphoreType.DMA((4,)),
                pltpu.SemaphoreType.DMA((8,)),
                pltpu.SemaphoreType.DMA((6,)),
            ],
            compiler_params=pltpu.CompilerParams(
                collective_id=0, has_side_effects=True, vmem_limit_bytes=50 * 2**20
            ),
            cost_estimate=pl.CostEstimate(
                flops=36 * pos * DH * DH * heads, bytes_accessed=16 * pos * width, transcendentals=0
            ),
            name="attention",
        )(queries, keys, values, log_decay, norm_gain.reshape(1, width), d_out)

    wide = P("ctx", "head")
    return jax.shard_map(
        local,
        mesh=mesh,
        in_specs=(wide, wide, wide, P("head", "ctx"), P("head"), wide),
        out_specs=(wide, wide, wide, wide),
        check_vma=False,
    )
```

time: 796 us -> 62.7 us (0.08)
  waiting for transfers between devices: 441 us -> 0 us
  blocking collectives: 188 us -> 0 us
  other arithmetic: 100 us -> 0 us
  Pallas kernels: 0 us -> 55.9 us
  matrix products: 25.9 us -> 0 us
  between operations: 14.9 us -> 0.65 us
  local copies, waits for them, and re-layouts: 20.1 us -> 5.92 us
    all_gather x2 -> x0, waiting for transfers between devices: 440 us -> none  [carried_in(): gathered = jax.tree.map(lambda a: lax.all_gather(a, axis), part)]
    unnamed x1 -> x0, blocking collectives: 183 us -> none
    add x63 -> x0, other arithmetic: 91.3 us -> none  [reverse_combine(): later[1] + later[0][:, None, None] * earlier[1]]
    pallas_call x0 -> x1, Pallas kernels: none -> 55.9 us  [local(): pl.pallas_call(functools.partial(kernel, n, heads, pos), out_shape=[wide]...]
    dot_general x12 -> x0, matrix products: 25.9 us -> none  [the longest x1 3.87 us: local(): jnp.einsum('htd,hte->hde', decayed_keys, value_h, preferred_element_type=...]
    unnamed x47 -> x10, local copies, waits for them, and re-layouts: 15.6 us -> 5.92 us
  transfers between devices with their start and end apart: 2 -> 0, of which waited for: 2 -> 0; matrix products, arithmetic and copies ran while one was open for 3% -> 0% of each run, Pallas kernels for 0% -> 0%
where the time goes in v1:
time: 62.7 us; the launch traced here: 62.4 us
  Pallas kernels  55.9 us (89%)
  local copies, waits for them, and re-layouts  5.92 us (9%)
  between operations  0.65 us (1%)
    pallas_call x1, Pallas kernels, local(): pl.pallas_call(functools.partial(kernel, n, heads, pos), out_shape=[wide]...  55.9 us
    unnamed x10, local copies, waits for them, and re-layouts  5.92 us

profile of v1, /device:TPU:0, one launch (start us, length us, event | category | flops | bytes accessed | tf_op | source)
XLA Modules:
  0.0 62.4 jit_solution(9221724952554511121)
XLA Ops:
  0.6 0.0 copy-start
  0.6 0.7 %copy-done = f32[16,256]{1,0:T(8,128)S(1)} copy-done((f32[16,256]{1,0:T(8,128)S(1)}, f32[16,256]{1,0:T(8,128)}, u32[]{:S(2)}) %copy-start) | copy-done | bytes 16408
  1.4 0.0 copy-start.1
  1.4 0.7 %copy-done.1 = f32[2048]{0:T(1024)S(1)} copy-done((f32[2048]{0:T(1024)S(1)}, f32[2048]{0:T(1024)}, u32[]{:S(2)}) %copy-start.1) | copy-done | bytes 8216
  2.0 55.9 %attention.1 = (bf16[256,2048]{1,0:T(8,128)(2,1)S(1)}, bf16[256,2048]{1,0:T(8,128)(2,1)S(1)}, bf16[256,2048]{1,0:T(8,128)(2,1)S(1)}, bf16[256,2048]{1,0:T(8,128)(2,1)}) custom-call(bf16[256,2048]{1,0:T(8,128)(2,1)} %q_hbm.1, bf16[256,2048]{1,0:T(8,128)(2,1)} %k_hbm.1, bf16[256,2048]{1,0:T(8,128)(2,1)} %v_hbm.1, f32[16,256]{1,0:T(8,128)S(1)} %copy-done, ...), custom_call_target="tpu_custom_call" | custom-call | flops 2415919104 | bytes 8388608 | tf_op jit(solution)/shard_map/attention/pallas_call | solution.py:316
  57.9 1.0 %copy.14 = bf16[256,2048]{1,0:T(8,128)(2,1)} copy(bf16[256,2048]{1,0:T(8,128)(2,1)S(1)} %get-tuple-element.8) | data formatting | bytes 2097152
  58.9 1.0 %copy.15 = bf16[256,2048]{1,0:T(8,128)(2,1)} copy(bf16[256,2048]{1,0:T(8,128)(2,1)S(1)} %get-tuple-element.9) | data formatting | bytes 2097152
  59.9 0.0 copy-start.2
  59.9 1.0 %copy.16 = bf16[256,2048]{1,0:T(8,128)(2,1)} copy(bf16[256,2048]{1,0:T(8,128)(2,1)S(1)} %get-tuple-element.10) | data formatting | bytes 2097152
  60.8 0.6 %copy-done.2 = bf16[256,2048]{1,0:T(8,128)(2,1)S(1)} copy-done((bf16[256,2048]{1,0:T(8,128)(2,1)S(1)}, bf16[256,2048]{1,0:T(8,128)(2,1)}, u32[]{:S(2)}) %copy-start.2) | copy-done | bytes 1048600
  61.5 1.0 %copy.17 = bf16[256,2048]{1,0:T(8,128)(2,1)} copy(bf16[256,2048]{1,0:T(8,128)(2,1)S(1)} %copy-done.2) | data formatting | bytes 2097152
Async XLA Ops:
  0.6 0.7 %copy-start = (f32[16,256]{1,0:T(8,128)S(1)}, f32[16,256]{1,0:T(8,128)}, u32[]{:S(2)}) copy-start(f32[16,256]{1,0:T(8,128)} %ld_hbm.1) | copy-start | bytes 49156
  1.4 0.7 %copy-start.1 = (f32[2048]{0:T(1024)S(1)}, f32[2048]{0:T(1024)}, u32[]{:S(2)}) copy-start(f32[2048]{0:T(1024)} %param.10) | copy-start | bytes 24580
  59.9 1.6 %copy-start.2 = (bf16[256,2048]{1,0:T(8,128)(2,1)S(1)}, bf16[256,2048]{1,0:T(8,128)(2,1)}, u32[]{:S(2)}) copy-start(bf16[256,2048]{1,0:T(8,128)(2,1)} %get-tuple-element.11) | copy-start | bytes 3145732

commit v2 on v1

v2 whole, which is shorter than its diff:
```python
import functools
import itertools

import jax
import jax.numpy as jnp
from jax import lax
from jax.experimental import pallas as pl
from jax.experimental.pallas import tpu as pltpu
from jax.sharding import PartitionSpec as P

DH = 128
EPSILON = 1e-06
SIDE = 4
SPLIT = (2, 2, 2)
HOPS = (0, 1, 2, 1)
MESH = pl.DeviceIdType.MESH
F32 = jnp.float32
BF16 = jnp.bfloat16
NN = ((1,), (0,))
NT = ((1,), (1,))
TN = ((0,), (0,))


def dot(a, b, dims):
    return lax.dot_general(a, b, (dims, ((), ())), preferred_element_type=F32)


def routes(place, group, split):
    per_axis = []
    for at, chosen, part in zip(place, group, split):
        steps = []
        for turn in range(SIDE // part):
            shift = (chosen - at) % part + part * turn
            hops = sum(HOPS[part * turn + i] for i in range(part)) / part
            steps.append(((at + shift) % SIDE, hops, turn == 0))
        per_axis.append(steps)
    found = []
    for steps in itertools.product(*per_axis):
        ctx, member = 0, 0
        for (at, _, _), part in zip(steps, split):
            ctx = ctx * SIDE + at
            member = member * (SIDE // part) + at // part
        found.append((sum(s[1] for s in steps), ctx, member, all(s[2] for s in steps)))
    found.sort(key=lambda r: -r[0])
    return [r[1:] for r in found]


def kernel(
    n, heads, pos,
    q_hbm, k_hbm, v_hbm, ld_hbm, gain_hbm, g_hbm,
    out, gq, gk, gv,
    q, k, v, g, ld, gain,
    cum, cumb, leadb, trailb, decay, weights, dk, dv, ql, qt,
    attn, gg, d_attn,
    s_send, s_recv, e_send, e_recv, t_send, t_recv, l_send, l_recv,
    totals, block_decay, sums, sums_in,
    in_sem, share_sem, group_sem, sum_sem,
):
    c = lax.axis_index("ctx")
    core = lax.axis_index("head")
    place = (c // (SIDE * SIDE), (c // SIDE) % SIDE, c % SIDE)
    rows = DH * heads // n
    per_head = n // heads
    groups = list(itertools.product(*(range(part) for part in SPLIT)))
    members = n // len(groups)
    group_heads = heads // len(groups)
    my_group, my_member = 0, 0
    for at, part in zip(place, SPLIT):
        my_group = my_group * part + at % part
        my_member = my_member * (SIDE // part) + at // part
    mine = my_group * members + my_member
    width = heads * DH

    loads = [
        pltpu.make_async_copy(src, dst, in_sem.at[i])
        for i, (src, dst) in enumerate(
            ((ld_hbm, ld), (k_hbm, k), (v_hbm, v), (q_hbm, q), (gain_hbm, gain), (g_hbm, g))
        )
    ]
    for load in loads:
        load.start()

    barrier = pltpu.get_barrier_semaphore()

    def greet(i, _):
        pl.semaphore_signal(
            barrier, inc=1, device_id=((c + i) % n, core), device_id_type=MESH
        )
        return 0

    lax.fori_loop(1, n, greet, 0)
    pl.semaphore_signal(barrier, inc=1, device_id=(c, 1 - core), device_id_type=MESH)

    def lanes(h):
        return pl.ds(h * DH, DH) if isinstance(h, int) else pl.ds(pl.multiple_of(h * DH, DH), DH)

    def shares(h):
        return pl.ds(h * per_head, per_head)

    def send(src, dst, sent, landed, dest, maybe_me):
        def away():
            pltpu.make_async_remote_copy(
                src_ref=src, dst_ref=dst, send_sem=sent, recv_sem=landed,
                device_id=(dest, core), device_id_type=MESH,
            ).start()

        if maybe_me:
            pl.when(dest != c)(away)

            @pl.when(dest == c)
            def _():
                pltpu.make_async_copy(src, dst, landed).start()
        else:
            away()

    def to_owners(src, dst, which, group):
        for dest, member, maybe_me in routes(place, groups[group], SPLIT):
            send(
                src.at[group * members + member], dst.at[c],
                share_sem.at[2 * which], share_sem.at[2 * which + 1], dest, maybe_me,
            )

    def from_owner(src, dst, which):
        for dest, _, maybe_me in routes(place, (0, 0, 0), (1, 1, 1)):
            send(
                src.at[dest], dst.at[mine],
                share_sem.at[4 + which], group_sem.at[which, my_group], dest, maybe_me,
            )

    def any_copy(ref, sent, landed):
        return pltpu.make_async_remote_copy(
            src_ref=ref, dst_ref=ref, send_sem=sent, recv_sem=landed,
            device_id=((c + 1) % n, core), device_id_type=MESH,
        )

    def owners_wait(dst, which):
        any_copy(dst, share_sem.at[2 * which], share_sem.at[2 * which + 1]).wait_recv()

    def group_wait(dst, which, group):
        any_copy(
            dst.at[pl.ds(group * members, members)],
            share_sem.at[4 + which], group_sem.at[which, group],
        ).wait_recv()

    def each(first, last, body, unroll):
        def step(h, _):
            body(h)
            return 0

        lax.fori_loop(first, last, step, 0, unroll=unroll)

    loads[0].wait()
    t_i = lax.broadcasted_iota(jnp.int32, (pos, pos), 0)
    s_i = lax.broadcasted_iota(jnp.int32, (pos, pos), 1)
    lower = jnp.where(t_i >= s_i, 1.0, 0.0).astype(BF16)
    ld_all = jnp.concatenate([ld[...], jnp.zeros((DH - heads, pos), F32)], axis=0)
    hi = ld_all.astype(BF16)
    rest = ld_all - hi.astype(F32)
    mid = rest.astype(BF16)
    low = (rest - mid.astype(F32)).astype(BF16)
    cum_t = dot(lower, hi, NT) + dot(lower, mid, NT) + dot(lower, low, NT)
    last = cum_t[pos - 1 : pos, :]
    trail_t = jnp.exp(last - cum_t)
    for h in range(heads):
        trailb[h] = jnp.broadcast_to(trail_t[:, h : h + 1], (pos, DH))
    my_row = totals.at[c // 8, c % 8]
    my_row[...] = last

    loads[1].wait()
    loads[2].wait()

    def own_state(h):
        keys = (k[:, lanes(h)].astype(F32) * trailb[h]).astype(BF16)
        dk[:, lanes(h)] = keys
        state = dot(keys, v[:, lanes(h)], TN).astype(BF16)
        s_send[shares(h)] = state.reshape(per_head, rows, DH)

    for group in range(len(groups)):
        each(group * group_heads, (group + 1) * group_heads, own_state, 2)
        if group == 0:
            pl.semaphore_wait(barrier, n)
            for i in range(1, 8):
                pltpu.make_async_remote_copy(
                    src_ref=my_row, dst_ref=my_row,
                    send_sem=sum_sem.at[2], recv_sem=sum_sem.at[3],
                    device_id=((c // 8) * 8 + (c + i) % 8, core), device_id_type=MESH,
                ).start()
        to_owners(s_send, s_recv, 0, group)

    cum_h = dot(hi, lower, NT) + dot(mid, lower, NT) + dot(low, lower, NT)
    cum[...] = cum_h[:heads]
    lead_t = jnp.exp(cum_t)
    for h in range(heads):
        cumb[h] = jnp.broadcast_to(cum_t[:, h : h + 1], (pos, DH))
        leadb[h] = jnp.broadcast_to(lead_t[:, h : h + 1], (pos, DH))

    loads[3].wait()

    def inside(h):
        scores = dot(q[:, lanes(h)], k[:, lanes(h)], NT)
        row = cum[pl.ds(h, 1), :]
        col = cumb[h]
        spread = jnp.concatenate([col, col], axis=1) - row
        d = jnp.exp(jnp.where(t_i >= s_i, spread, -1e30))
        decay[h] = d
        w = (scores * d).astype(BF16)
        weights[h] = w
        attn[:, lanes(h)] = dot(w, v[:, lanes(h)], NN)
        lead_q = (q[:, lanes(h)].astype(F32) * leadb[h]).astype(BF16)
        ql[:, lanes(h)] = lead_q
        qt[h] = lead_q.T

    each(0, heads // 4, inside, 2)

    any_copy(totals.at[0, pl.ds(0, 7)], sum_sem.at[2], sum_sem.at[3]).wait()
    for i in range(1, 8):
        pltpu.make_async_remote_copy(
            src_ref=totals.at[c // 8], dst_ref=totals.at[c // 8],
            send_sem=sum_sem.at[4], recv_sem=sum_sem.at[5],
            device_id=((c // 8 + i) % 8 * 8 + c % 8, core), device_id_type=MESH,
        ).start()

    each(heads // 4, heads // 2, inside, 2)

    any_copy(totals.at[pl.ds(0, 7)], sum_sem.at[4], sum_sem.at[5]).wait()
    every = totals[...].reshape(n, DH)
    lane_i = lax.broadcasted_iota(jnp.int32, (n, DH), 1)
    total = jnp.sum(jnp.where(lane_i == mine // per_head, every, 0.0), axis=1, keepdims=True)
    block_decay[...] = jnp.broadcast_to(jnp.exp(total), (n, DH))

    def scan(src, dst, reverse):
        def one(i, state):
            j = n - 1 - i if reverse else i
            dst[j] = state.astype(BF16)
            return state * block_decay[pl.ds(j, 1), :] + src[j].astype(F32)

        lax.fori_loop(0, n, one, jnp.zeros((rows, DH), F32), unroll=8)

    owners_wait(s_recv, 0)
    scan(s_recv, e_send, False)
    from_owner(e_send, e_recv, 0)

    each(heads // 2, heads, inside, 2)
    loads[4].wait()
    loads[5].wait()

    def prepare(h):
        gg[:, lanes(h)] = gain[:, lanes(h)] * g[:, lanes(h)].astype(F32)
        dv[:, lanes(h)] = (v[:, lanes(h)].astype(F32) * trailb[h]).astype(BF16)

    each(0, heads, prepare, 2)

    def attend(h, carry):
        squares, inner = carry
        entering = e_recv[shares(h)].reshape(DH, DH)
        a = attn[:, lanes(h)] + dot(ql[:, lanes(h)], entering, NN)
        attn[:, lanes(h)] = a
        return squares + a * a, inner + a * gg[:, lanes(h)]

    squares = inner = jnp.zeros((pos, DH), F32)
    for group in range(len(groups)):
        group_wait(e_recv, 0, group)
        squares, inner = lax.fori_loop(
            group * group_heads, (group + 1) * group_heads, attend, (squares, inner), unroll=2
        )
    squares = jnp.sum(squares, axis=1, keepdims=True)
    inner = jnp.sum(inner, axis=1, keepdims=True)
    half_i = lax.broadcasted_iota(jnp.int32, (pos, DH), 1)
    sums[...] = jnp.where(half_i < DH // 2, squares, inner)
    swap = pltpu.make_async_remote_copy(
        src_ref=sums, dst_ref=sums_in, send_sem=sum_sem.at[0], recv_sem=sum_sem.at[1],
        device_id=(c, 1 - core), device_id_type=MESH,
    )
    swap.start()
    swap.wait()
    both = sums[...] + sums_in[...]
    full = 2 * width
    scale = lax.rsqrt(both[:, 0:1] / full + EPSILON)
    pull = scale * scale * scale * (both[:, DH - 1 : DH] / full)
    sums[...] = jnp.broadcast_to(scale, (pos, DH))
    sums_in[...] = jnp.broadcast_to(pull, (pos, DH))

    def own_grad(h):
        d = (sums[...] * gg[:, lanes(h)] - attn[:, lanes(h)] * sums_in[...]).astype(BF16)
        d_attn[:, lanes(h)] = d
        state = dot(qt[h], d, NN).astype(BF16)
        t_send[shares(h)] = state.reshape(per_head, rows, DH)

    for group in range(len(groups)):
        each(group * group_heads, (group + 1) * group_heads, own_grad, 2)
        to_owners(t_send, t_recv, 1, group)

    def gradients(h):
        d = d_attn[:, lanes(h)]
        out[:, lanes(h)] = (attn[:, lanes(h)] * sums[...] * gain[:, lanes(h)]).astype(BF16)
        w = weights[h]
        gw = (dot(d, v[:, lanes(h)], NT) * decay[h]).astype(BF16)
        entering = e_recv[shares(h)].reshape(DH, DH)
        gq[:, lanes(h)] = (
            leadb[h] * dot(d, entering, NT) + dot(gw, k[:, lanes(h)], NN)
        ).astype(BF16)
        attn[:, lanes(h)] = dot(gw, q[:, lanes(h)], TN)
        decay[h, :, 0:DH] = dot(w, d, TN)

    each(0, heads // 2, gradients, 1)
    owners_wait(t_recv, 1)
    scan(t_recv, l_send, True)
    from_owner(l_send, l_recv, 1)
    each(heads // 2, heads, gradients, 1)

    def finish(h):
        leaving = l_recv[shares(h)].reshape(DH, DH)
        gk[:, lanes(h)] = (attn[:, lanes(h)] + dot(dv[:, lanes(h)], leaving, NT)).astype(BF16)
        gv[:, lanes(h)] = (decay[h, :, 0:DH] + dot(dk[:, lanes(h)], leaving, NN)).astype(BF16)

    for group in range(len(groups)):
        group_wait(l_recv, 1, group)
        each(group * group_heads, (group + 1) * group_heads, finish, 2)

    for which, ref in enumerate((s_send, t_send, e_send, l_send)):
        any_copy(ref.at[pl.ds(0, n - 1)], share_sem.at[(0, 2, 4, 5)[which]], share_sem.at[1]).wait_send()


def write_out(*refs):
    copies = [
        pltpu.make_async_copy(src, dst, refs[8].at[i])
        for i, (src, dst) in enumerate(zip(refs[:4], refs[4:8]))
    ]
    for copy in copies:
        copy.start()
    for copy in copies:
        copy.wait()


def solution(mesh):
    n = mesh.shape["ctx"]

    def local(queries, keys, values, log_decay, norm_gain, d_out):
        pos, width = queries.shape
        heads = width // DH
        rows = DH * heads // n
        wide = jax.ShapeDtypeStruct((pos, width), BF16)
        hbm = pl.BlockSpec(memory_space=pltpu.HBM)
        vmem = pl.BlockSpec(memory_space=pltpu.VMEM)
        shares = pltpu.VMEM((n, rows, DH), BF16)
        columns = pltpu.VMEM((heads, pos, DH), F32)
        flat = pltpu.VMEM((pos, width), BF16)
        flat_f32 = pltpu.VMEM((pos, width), F32)
        small = pltpu.VMEM((pos, DH), F32)
        held = pl.pallas_call(
            functools.partial(kernel, n, heads, pos),
            out_shape=[pltpu.VMEM((pos, width), BF16)] * 4,
            in_specs=[hbm] * 6,
            out_specs=[vmem] * 4,
            scratch_shapes=[
                flat, flat, flat, flat,
                pltpu.VMEM((heads, pos), F32),
                pltpu.VMEM((1, width), F32),
                pltpu.VMEM((heads, pos), F32),
                columns, columns, columns,
                pltpu.VMEM((heads, pos, pos), F32),
                pltpu.VMEM((heads, pos, pos), BF16),
                flat, flat, flat,
                pltpu.VMEM((heads, DH, pos), BF16),
                flat_f32, flat_f32, flat,
                shares, shares, shares, shares, shares, shares, shares, shares,
                pltpu.VMEM((8, n // 8, 1, DH), F32),
                pltpu.VMEM((n, DH), F32),
                small, small,
                pltpu.SemaphoreType.DMA((6,)),
                pltpu.SemaphoreType.DMA((6,)),
                pltpu.SemaphoreType.DMA((2, SPLIT[0] * SPLIT[1] * SPLIT[2])),
                pltpu.SemaphoreType.DMA((6,)),
            ],
            compiler_params=pltpu.CompilerParams(
                collective_id=0, has_side_effects=True, vmem_limit_bytes=44 * 2**20
            ),
            cost_estimate=pl.CostEstimate(
                flops=36 * pos * DH * DH * heads, bytes_accessed=16 * pos * width, transcendentals=0
            ),
            name="attention",
        )(*(pltpu.with_memory_space_constraint(a, pltpu.HBM) for a in (queries, keys, values, log_decay, norm_gain.reshape(1, width), d_out)))
        return pl.pallas_call(
            write_out,
            out_shape=[wide] * 4,
            in_specs=[pl.BlockSpec(memory_space=pl.ANY)] * 4,
            out_specs=[hbm] * 4,
            scratch_shapes=[pltpu.SemaphoreType.DMA((4,))],
            compiler_params=pltpu.CompilerParams(vmem_limit_bytes=16 * 2**20),
            name="write_out",
        )(*(pltpu.with_memory_space_constraint(a, pltpu.VMEM) for a in held))

    wide = P("ctx", "head")
    return jax.shard_map(
        local,
        mesh=mesh,
        in_specs=(wide, wide, wide, P("head", "ctx"), P("head"), wide),
        out_specs=(wide, wide, wide, wide),
        check_vma=False,
    )
```

time: 62.7 us -> 54 us (0.86)
  local copies, waits for them, and re-layouts: 5.92 us -> 0 us
  Pallas kernels: 55.9 us -> 53.2 us
    unnamed x10 -> x0, local copies, waits for them, and re-layouts: 5.92 us -> none
    pallas_call x1 -> x2, Pallas kernels: 55.9 us -> 53.2 us  [the longest x1 51.2 us: local(): pl.pallas_call(functools.partial(kernel, n, heads, pos), out_shape=[pltpu...]
where the time goes in v2:
time: 54 us; the launch traced here: 53.9 us
  Pallas kernels  53.2 us (99%)
  between operations  0.64 us (1%)
    pallas_call x1, Pallas kernels, local(): pl.pallas_call(functools.partial(kernel, n, heads, pos), out_shape=[pltpu...  51.2 us
    pallas_call x1, Pallas kernels, local(): pl.pallas_call(write_out, out_shape=[wide] * 4, in_specs=[pl.BlockSpec(me...  2.04 us

profile of v2, /device:TPU:0, one launch (start us, length us, event | category | flops | bytes accessed | tf_op | source)
XLA Modules:
  0.0 53.9 jit_solution(16467546498863595012)
XLA Ops:
  0.6 51.2 %attention.1 = (bf16[256,2048]{1,0:T(8,128)(2,1)S(1)}, bf16[256,2048]{1,0:T(8,128)(2,1)S(1)}, bf16[256,2048]{1,0:T(8,128)(2,1)S(1)}, bf16[256,2048]{1,0:T(8,128)(2,1)S(1)}) custom-call(bf16[256,2048]{1,0:T(8,128)(2,1)} %q_hbm.1, bf16[256,2048]{1,0:T(8,128)(2,1)} %k_hbm.1, bf16[256,2048]{1,0:T(8,128)(2,1)} %v_hbm.1, f32[16,256]{1,0:T(8,128)} %ld_hbm.1, ...), custom_call_target="tpu_custom_call" | custom-call | flops 2415919104 | bytes 8388608 | tf_op jit(solution)/shard_map/attention/pallas_call | solution.py:350
  51.8 2.0 %write_out.1 = (bf16[256,2048]{1,0:T(8,128)(2,1)}, bf16[256,2048]{1,0:T(8,128)(2,1)}, bf16[256,2048]{1,0:T(8,128)(2,1)}, bf16[256,2048]{1,0:T(8,128)(2,1)}) custom-call(bf16[256,2048]{1,0:T(8,128)(2,1)S(1)} %get-tuple-element.8.refs_0_, bf16[256,2048]{1,0:T(8,128)(2,1)S(1)} %get-tuple-element.9.refs_1_, bf16[256,2048]{1,0:T(8,128)(2,1)S(1)} %get-tuple-element.10.refs_2_, ...), custom_call_target="tpu_custom_call" | custom-call | tf_op jit(solution)/shard_map/write_out/pallas_call | solution.py:383

commit v3 on v2

--- a/solution.py
+++ b/solution.py
@@ -11,7 +11,7 @@
 DH = 128
 EPSILON = 1e-06
 SIDE = 4
-SPLIT = (2, 2, 2)
+SPLIT = (1, 2, 2)
 HOPS = (0, 1, 2, 1)
 MESH = pl.DeviceIdType.MESH
 F32 = jnp.float32
@@ -45,15 +45,27 @@
     return [r[1:] for r in found]
 
 
+def parts_of(a):
+    hi = a.astype(BF16)
+    rest = a - hi.astype(F32)
+    mid = rest.astype(BF16)
+    return [hi, mid, (rest - mid.astype(F32)).astype(BF16)]
+
+
+def along_lanes(a):
+    ones = jnp.ones((8, a.shape[1]), BF16)
+    return sum(dot(ones, part, NT) for part in parts_of(a))
+
+
 def kernel(
     n, heads, pos,
     q_hbm, k_hbm, v_hbm, ld_hbm, gain_hbm, g_hbm,
     out, gq, gk, gv,
     q, k, v, g, ld, gain,
-    cum, cumb, leadb, trailb, decay, weights, dk, dv, ql, qt,
+    cum, trail_h, kt, cumb, leadb, trailb, decay, weights, dk, dv, ql, qt,
     attn, gg, d_attn,
     s_send, s_recv, e_send, e_recv, t_send, t_recv, l_send, l_recv,
-    totals, block_decay, sums, sums_in,
+    totals, block_decay, sums, sums_in, scaleb, pullb,
     in_sem, share_sem, group_sem, sum_sem,
 ):
     c = lax.axis_index("ctx")
@@ -149,50 +161,61 @@
 
         lax.fori_loop(first, last, step, 0, unroll=unroll)
 
-    loads[0].wait()
     t_i = lax.broadcasted_iota(jnp.int32, (pos, pos), 0)
     s_i = lax.broadcasted_iota(jnp.int32, (pos, pos), 1)
     lower = jnp.where(t_i >= s_i, 1.0, 0.0).astype(BF16)
-    ld_all = jnp.concatenate([ld[...], jnp.zeros((DH - heads, pos), F32)], axis=0)
+
+    loads[0].wait()
+    ld_all = ld[...]
     hi = ld_all.astype(BF16)
     rest = ld_all - hi.astype(F32)
     mid = rest.astype(BF16)
     low = (rest - mid.astype(F32)).astype(BF16)
-    cum_t = dot(lower, hi, NT) + dot(lower, mid, NT) + dot(lower, low, NT)
-    last = cum_t[pos - 1 : pos, :]
-    trail_t = jnp.exp(last - cum_t)
-    for h in range(heads):
-        trailb[h] = jnp.broadcast_to(trail_t[:, h : h + 1], (pos, DH))
+    parts = jnp.concatenate([hi, mid, low], axis=0)
+    summed = dot(parts, lower, NT)
+    cum_h = summed[:heads] + summed[heads : 2 * heads] + summed[2 * heads :]
+    cum[...] = cum_h
+    trail_h[...] = jnp.exp(cum_h[:, pos - 1 :] - cum_h)
     my_row = totals.at[c // 8, c % 8]
-    my_row[...] = last
+    padded = jnp.concatenate([cum_h[:, pos - DH :], jnp.zeros((DH - heads, DH), F32)], axis=0)
+    my_row[...] = padded.T[DH - 1 :, :]
 
     loads[1].wait()
+
+    def turn(h):
+        kt[h] = k[:, lanes(h)].T
+
+    each(0, heads, turn, 4)
     loads[2].wait()
 
     def own_state(h):
-        keys = (k[:, lanes(h)].astype(F32) * trailb[h]).astype(BF16)
-        dk[:, lanes(h)] = keys
-        state = dot(keys, v[:, lanes(h)], TN).astype(BF16)
+        keys = (kt[h].astype(F32) * trail_h[pl.ds(h, 1), :]).astype(BF16)
+        state = dot(keys, v[:, lanes(h)], NN).astype(BF16)
         s_send[shares(h)] = state.reshape(per_head, rows, DH)
 
+    def send_totals():
+        for i in range(1, 8):
+            pltpu.make_async_remote_copy(
+                src_ref=my_row, dst_ref=my_row,
+                send_sem=sum_sem.at[2], recv_sem=sum_sem.at[3],
+                device_id=((c // 8) * 8 + (c + i) % 8, core), device_id_type=MESH,
+            ).start()
+
+    each(0, heads, own_state, 4)
+    pl.semaphore_wait(barrier, n)
+    send_totals()
     for group in range(len(groups)):
-        each(group * group_heads, (group + 1) * group_heads, own_state, 2)
-        if group == 0:
-            pl.semaphore_wait(barrier, n)
-            for i in range(1, 8):
-                pltpu.make_async_remote_copy(
-                    src_ref=my_row, dst_ref=my_row,
-                    send_sem=sum_sem.at[2], recv_sem=sum_sem.at[3],
-                    device_id=((c // 8) * 8 + (c + i) % 8, core), device_id_type=MESH,
-                ).start()
         to_owners(s_send, s_recv, 0, group)
 
-    cum_h = dot(hi, lower, NT) + dot(mid, lower, NT) + dot(low, lower, NT)
-    cum[...] = cum_h[:heads]
+    parts = jnp.concatenate([parts, jnp.zeros((DH - 3 * heads, pos), BF16)], axis=0)
+    summed = dot(lower, parts, NT)
+    cum_t = summed[:, :heads] + summed[:, heads : 2 * heads] + summed[:, 2 * heads : 3 * heads]
+    trail_t = jnp.exp(cum_t[pos - 1 :, :] - cum_t)
     lead_t = jnp.exp(cum_t)
     for h in range(heads):
         cumb[h] = jnp.broadcast_to(cum_t[:, h : h + 1], (pos, DH))
         leadb[h] = jnp.broadcast_to(lead_t[:, h : h + 1], (pos, DH))
+        trailb[h] = jnp.broadcast_to(trail_t[:, h : h + 1], (pos, DH))
 
     loads[3].wait()
 
@@ -246,6 +269,7 @@
 
     def prepare(h):
         gg[:, lanes(h)] = gain[:, lanes(h)] * g[:, lanes(h)].astype(F32)
+        dk[:, lanes(h)] = (k[:, lanes(h)].astype(F32) * trailb[h]).astype(BF16)
         dv[:, lanes(h)] = (v[:, lanes(h)].astype(F32) * trailb[h]).astype(BF16)
 
     each(0, heads, prepare, 2)
@@ -261,38 +285,41 @@
     for group in range(len(groups)):
         group_wait(e_recv, 0, group)
         squares, inner = lax.fori_loop(
-            group * group_heads, (group + 1) * group_heads, attend, (squares, inner), unroll=2
+            group * group_heads, (group + 1) * group_heads, attend, (squares, inner), unroll=4
         )
-    squares = jnp.sum(squares, axis=1, keepdims=True)
-    inner = jnp.sum(inner, axis=1, keepdims=True)
-    half_i = lax.broadcasted_iota(jnp.int32, (pos, DH), 1)
-    sums[...] = jnp.where(half_i < DH // 2, squares, inner)
+    sums[...] = jnp.concatenate([along_lanes(squares), along_lanes(inner)], axis=0)
     swap = pltpu.make_async_remote_copy(
         src_ref=sums, dst_ref=sums_in, send_sem=sum_sem.at[0], recv_sem=sum_sem.at[1],
         device_id=(c, 1 - core), device_id_type=MESH,
     )
     swap.start()
     swap.wait()
-    both = sums[...] + sums_in[...]
-    full = 2 * width
-    scale = lax.rsqrt(both[:, 0:1] / full + EPSILON)
-    pull = scale * scale * scale * (both[:, DH - 1 : DH] / full)
-    sums[...] = jnp.broadcast_to(scale, (pos, DH))
-    sums_in[...] = jnp.broadcast_to(pull, (pos, DH))
+    both = (sums[...] + sums_in[...]) / (2 * width)
+    scale = lax.rsqrt(both[:8] + EPSILON)
+    pull = scale * scale * scale * both[8:]
+    part_i = lax.broadcasted_iota(jnp.int32, (48, 2 * DH), 0)
+    lane_i = lax.broadcasted_iota(jnp.int32, (48, 2 * DH), 1)
+    chosen = (part_i % 8 == 0) & ((part_i < 24) == (lane_i < DH))
+    both = dot(
+        jnp.concatenate(parts_of(scale) + parts_of(pull), axis=0),
+        jnp.where(chosen, 1.0, 0.0).astype(BF16), TN,
+    )
+    scaleb[...] = both[:, :DH]
+    pullb[...] = both[:, DH:]
 
     def own_grad(h):
-        d = (sums[...] * gg[:, lanes(h)] - attn[:, lanes(h)] * sums_in[...]).astype(BF16)
+        d = (scaleb[...] * gg[:, lanes(h)] - attn[:, lanes(h)] * pullb[...]).astype(BF16)
         d_attn[:, lanes(h)] = d
         state = dot(qt[h], d, NN).astype(BF16)
         t_send[shares(h)] = state.reshape(per_head, rows, DH)
 
     for group in range(len(groups)):
-        each(group * group_heads, (group + 1) * group_heads, own_grad, 2)
+        each(group * group_heads, (group + 1) * group_heads, own_grad, 4)
         to_owners(t_send, t_recv, 1, group)
 
     def gradients(h):
         d = d_attn[:, lanes(h)]
-        out[:, lanes(h)] = (attn[:, lanes(h)] * sums[...] * gain[:, lanes(h)]).astype(BF16)
+        out[:, lanes(h)] = (attn[:, lanes(h)] * scaleb[...] * gain[:, lanes(h)]).astype(BF16)
         w = weights[h]
         gw = (dot(d, v[:, lanes(h)], NT) * decay[h]).astype(BF16)
         entering = e_recv[shares(h)].reshape(DH, DH)
@@ -315,7 +342,7 @@
 
     for group in range(len(groups)):
         group_wait(l_recv, 1, group)
-        each(group * group_heads, (group + 1) * group_heads, finish, 2)
+        each(group * group_heads, (group + 1) * group_heads, finish, 4)
 
     for which, ref in enumerate((s_send, t_send, e_send, l_send)):
         any_copy(ref.at[pl.ds(0, n - 1)], share_sem.at[(0, 2, 4, 5)[which]], share_sem.at[1]).wait_send()
@@ -357,6 +384,8 @@
                 pltpu.VMEM((heads, pos), F32),
                 pltpu.VMEM((1, width), F32),
                 pltpu.VMEM((heads, pos), F32),
+                pltpu.VMEM((heads, pos), F32),
+                pltpu.VMEM((heads, DH, pos), BF16),
                 columns, columns, columns,
                 pltpu.VMEM((heads, pos, pos), F32),
                 pltpu.VMEM((heads, pos, pos), BF16),
@@ -366,6 +395,8 @@
                 shares, shares, shares, shares, shares, shares, shares, shares,
                 pltpu.VMEM((8, n // 8, 1, DH), F32),
                 pltpu.VMEM((n, DH), F32),
+                pltpu.VMEM((16, pos), F32),
+                pltpu.VMEM((16, pos), F32),
                 small, small,
                 pltpu.SemaphoreType.DMA((6,)),
                 pltpu.SemaphoreType.DMA((6,)),

time: 54 us -> 53.1 us (0.983)
  Pallas kernels: 53.2 us -> 51.9 us
    pallas_call x1, Pallas kernels: 51.2 us -> 49.9 us  [local(): pl.pallas_call(functools.partial(kernel, n, heads, pos), out_shape=[pltpu...]
where the time goes in v3:
time: 53.1 us; the launch traced here: 52.6 us
  Pallas kernels  51.9 us (98%)
  between operations  0.64 us (1%)
    pallas_call x1, Pallas kernels, local(): pl.pallas_call(functools.partial(kernel, n, heads, pos), out_shape=[pltpu...  49.9 us
    pallas_call x1, Pallas kernels, local(): pl.pallas_call(write_out, out_shape=[wide] * 4, in_specs=[pl.BlockSpec(me...  2.04 us

profile of v3, /device:TPU:0, one launch (start us, length us, event | category | flops | bytes accessed | tf_op | source)
XLA Modules:
  0.0 52.6 jit_solution(9047232889519674742)
XLA Ops:
  0.6 49.9 %attention.1 = (bf16[256,2048]{1,0:T(8,128)(2,1)S(1)}, bf16[256,2048]{1,0:T(8,128)(2,1)S(1)}, bf16[256,2048]{1,0:T(8,128)(2,1)S(1)}, bf16[256,2048]{1,0:T(8,128)(2,1)S(1)}) custom-call(bf16[256,2048]{1,0:T(8,128)(2,1)} %q_hbm.1, bf16[256,2048]{1,0:T(8,128)(2,1)} %k_hbm.1, bf16[256,2048]{1,0:T(8,128)(2,1)} %v_hbm.1, f32[16,256]{1,0:T(8,128)} %ld_hbm.1, ...), custom_call_target="tpu_custom_call" | custom-call | flops 2415919104 | bytes 8388608 | tf_op jit(solution)/shard_map/attention/pallas_call | solution.py:377
  50.5 2.0 %write_out.1 = (bf16[256,2048]{1,0:T(8,128)(2,1)}, bf16[256,2048]{1,0:T(8,128)(2,1)}, bf16[256,2048]{1,0:T(8,128)(2,1)}, bf16[256,2048]{1,0:T(8,128)(2,1)}) custom-call(bf16[256,2048]{1,0:T(8,128)(2,1)S(1)} %get-tuple-element.8.refs_0_, bf16[256,2048]{1,0:T(8,128)(2,1)S(1)} %get-tuple-element.9.refs_1_, bf16[256,2048]{1,0:T(8,128)(2,1)S(1)} %get-tuple-element.10.refs_2_, ...), custom_call_target="tpu_custom_call" | custom-call | tf_op jit(solution)/shard_map/write_out/pallas_call | solution.py:414

commit v4 on v3

--- a/solution.py
+++ b/solution.py
@@ -12,6 +12,7 @@
 EPSILON = 1e-06
 SIDE = 4
 SPLIT = (1, 2, 2)
+PAIR = 2
 HOPS = (0, 1, 2, 1)
 MESH = pl.DeviceIdType.MESH
 F32 = jnp.float32
@@ -282,10 +283,12 @@
         return squares + a * a, inner + a * gg[:, lanes(h)]
 
     squares = inner = jnp.zeros((pos, DH), F32)
-    for group in range(len(groups)):
-        group_wait(e_recv, 0, group)
+    for group in range(0, len(groups), PAIR):
+        for i in range(PAIR):
+            group_wait(e_recv, 0, group + i)
         squares, inner = lax.fori_loop(
-            group * group_heads, (group + 1) * group_heads, attend, (squares, inner), unroll=4
+            group * group_heads, (group + PAIR) * group_heads, attend, (squares, inner),
+            unroll=PAIR * group_heads,
         )
     sums[...] = jnp.concatenate([along_lanes(squares), along_lanes(inner)], axis=0)
     swap = pltpu.make_async_remote_copy(
@@ -313,9 +316,10 @@
         state = dot(qt[h], d, NN).astype(BF16)
         t_send[shares(h)] = state.reshape(per_head, rows, DH)
 
-    for group in range(len(groups)):
-        each(group * group_heads, (group + 1) * group_heads, own_grad, 4)
-        to_owners(t_send, t_recv, 1, group)
+    for group in range(0, len(groups), PAIR):
+        each(group * group_heads, (group + PAIR) * group_heads, own_grad, PAIR * group_heads)
+        for i in range(PAIR):
+            to_owners(t_send, t_recv, 1, group + i)
 
     def gradients(h):
         d = d_attn[:, lanes(h)]
@@ -340,9 +344,10 @@
         gk[:, lanes(h)] = (attn[:, lanes(h)] + dot(dv[:, lanes(h)], leaving, NT)).astype(BF16)
         gv[:, lanes(h)] = (decay[h, :, 0:DH] + dot(dk[:, lanes(h)], leaving, NN)).astype(BF16)
 
-    for group in range(len(groups)):
-        group_wait(l_recv, 1, group)
-        each(group * group_heads, (group + 1) * group_heads, finish, 4)
+    for group in range(0, len(groups), PAIR):
+        for i in range(PAIR):
+            group_wait(l_recv, 1, group + i)
+        each(group * group_heads, (group + PAIR) * group_heads, finish, PAIR * group_heads)
 
     for which, ref in enumerate((s_send, t_send, e_send, l_send)):
         any_copy(ref.at[pl.ds(0, n - 1)], share_sem.at[(0, 2, 4, 5)[which]], share_sem.at[1]).wait_send()

time: 53.1 us -> 52.5 us (0.989)
  no operation moved by 1% of the time
where the time goes in v4:
time: 52.5 us; the launch traced here: 52.4 us
  Pallas kernels  51.7 us (98%)
  between operations  0.64 us (1%)
    pallas_call x1, Pallas kernels, local(): pl.pallas_call(functools.partial(kernel, n, heads, pos), out_shape=[pltpu...  49.7 us
    pallas_call x1, Pallas kernels, local(): pl.pallas_call(write_out, out_shape=[wide] * 4, in_specs=[pl.BlockSpec(me...  2.04 us

profile of v4, /device:TPU:0, one launch (start us, length us, event | category | flops | bytes accessed | tf_op | source)
XLA Modules:
  0.0 52.4 jit_solution(13380213995220560996)
XLA Ops:
  0.6 49.7 %attention.1 = (bf16[256,2048]{1,0:T(8,128)(2,1)S(1)}, bf16[256,2048]{1,0:T(8,128)(2,1)S(1)}, bf16[256,2048]{1,0:T(8,128)(2,1)S(1)}, bf16[256,2048]{1,0:T(8,128)(2,1)S(1)}) custom-call(bf16[256,2048]{1,0:T(8,128)(2,1)} %q_hbm.1, bf16[256,2048]{1,0:T(8,128)(2,1)} %k_hbm.1, bf16[256,2048]{1,0:T(8,128)(2,1)} %v_hbm.1, f32[16,256]{1,0:T(8,128)} %ld_hbm.1, ...), custom_call_target="tpu_custom_call" | custom-call | flops 2415919104 | bytes 8388608 | tf_op jit(solution)/shard_map/attention/pallas_call | solution.py:382
  50.3 2.0 %write_out.1 = (bf16[256,2048]{1,0:T(8,128)(2,1)}, bf16[256,2048]{1,0:T(8,128)(2,1)}, bf16[256,2048]{1,0:T(8,128)(2,1)}, bf16[256,2048]{1,0:T(8,128)(2,1)}) custom-call(bf16[256,2048]{1,0:T(8,128)(2,1)S(1)} %get-tuple-element.8.refs_0_, bf16[256,2048]{1,0:T(8,128)(2,1)S(1)} %get-tuple-element.9.refs_1_, bf16[256,2048]{1,0:T(8,128)(2,1)S(1)} %get-tuple-element.10.refs_2_, ...), custom_call_target="tpu_custom_call" | custom-call | tf_op jit(solution)/shard_map/write_out/pallas_call | solution.py:419

commit v5 on v4

--- a/solution.py
+++ b/solution.py
@@ -234,7 +234,7 @@
         ql[:, lanes(h)] = lead_q
         qt[h] = lead_q.T
 
-    each(0, heads // 4, inside, 2)
+    each(0, heads // 8, inside, 2)
 
     any_copy(totals.at[0, pl.ds(0, 7)], sum_sem.at[2], sum_sem.at[3]).wait()
     for i in range(1, 8):
@@ -244,7 +244,7 @@
             device_id=((c // 8 + i) % 8 * 8 + c % 8, core), device_id_type=MESH,
         ).start()
 
-    each(heads // 4, heads // 2, inside, 2)
+    each(heads // 8, heads // 2, inside, 2)
 
     any_copy(totals.at[pl.ds(0, 7)], sum_sem.at[4], sum_sem.at[5]).wait()
     every = totals[...].reshape(n, DH)
@@ -258,7 +258,7 @@
             dst[j] = state.astype(BF16)
             return state * block_decay[pl.ds(j, 1), :] + src[j].astype(F32)
 
-        lax.fori_loop(0, n, one, jnp.zeros((rows, DH), F32), unroll=8)
+        lax.fori_loop(0, n, one, jnp.zeros((rows, DH), F32), unroll=16)
 
     owners_wait(s_recv, 0)
     scan(s_recv, e_send, False)

time: 52.5 us -> 52.4 us (level)
  no operation moved by 1% of the time
where the time goes in v5:
time: 52.4 us; the launch traced here: 52.3 us
  Pallas kernels  51.7 us (99%)
  between operations  0.64 us (1%)
    pallas_call x1, Pallas kernels, local(): pl.pallas_call(functools.partial(kernel, n, heads, pos), out_shape=[pltpu...  49.6 us
    pallas_call x1, Pallas kernels, local(): pl.pallas_call(write_out, out_shape=[wide] * 4, in_specs=[pl.BlockSpec(me...  2.04 us

profile of v5, /device:TPU:0, one launch (start us, length us, event | category | flops | bytes accessed | tf_op | source)
XLA Modules:
  0.0 52.3 jit_solution(11279050217403950887)
XLA Ops:
  0.6 49.6 %attention.1 = (bf16[256,2048]{1,0:T(8,128)(2,1)S(1)}, bf16[256,2048]{1,0:T(8,128)(2,1)S(1)}, bf16[256,2048]{1,0:T(8,128)(2,1)S(1)}, bf16[256,2048]{1,0:T(8,128)(2,1)S(1)}) custom-call(bf16[256,2048]{1,0:T(8,128)(2,1)} %q_hbm.1, bf16[256,2048]{1,0:T(8,128)(2,1)} %k_hbm.1, bf16[256,2048]{1,0:T(8,128)(2,1)} %v_hbm.1, f32[16,256]{1,0:T(8,128)} %ld_hbm.1, ...), custom_call_target="tpu_custom_call" | custom-call | flops 2415919104 | bytes 8388608 | tf_op jit(solution)/shard_map/attention/pallas_call | solution.py:382
  50.3 2.0 %write_out.1 = (bf16[256,2048]{1,0:T(8,128)(2,1)}, bf16[256,2048]{1,0:T(8,128)(2,1)}, bf16[256,2048]{1,0:T(8,128)(2,1)}, bf16[256,2048]{1,0:T(8,128)(2,1)}) custom-call(bf16[256,2048]{1,0:T(8,128)(2,1)S(1)} %get-tuple-element.8.refs_0_, bf16[256,2048]{1,0:T(8,128)(2,1)S(1)} %get-tuple-element.9.refs_1_, bf16[256,2048]{1,0:T(8,128)(2,1)S(1)} %get-tuple-element.10.refs_2_, ...), custom_call_target="tpu_custom_call" | custom-call | tf_op jit(solution)/shard_map/write_out/pallas_call | solution.py:419
